TPU v7x, 32 devices: a whole 2x2x4 slice. The times are simulated.
32 devices in a mesh: mol: 8 (over y, x, core), frag: 4 (over z).
Axes of the slice: x: 2, y: 2, z: 4, core: 2. Of those that a mesh axis runs over, the one named last changes fastest.
Arguments:
- counts: bfloat16 [16384, 16384], P('mol', 'frag'), may hold values from 0 to 16, as said below
- mol_factor: bfloat16 [16384, 256], P('mol', 'frag'), may hold values from 0.0049 to 2, as said below
- frag_factor: bfloat16 [256, 16384], P('mol', 'frag'), may hold values from 0.0014 to 0.61, as said below
Outputs:
- new_mol: bfloat16 [16384, 256], P('mol', 'frag')
- new_frag: bfloat16 [256, 16384], P('mol', 'frag')
Inputs may be any that keep to these rules, and one draw needn't show every extreme that they name: `counts`: whole numbers, held exactly. `mol_factor`: positive entries. `frag_factor`: positive entries.
All inputs are finite; a program needn't handle non-finite values.
Results may differ from a plain program's by a relative error of at most 0.0034.
Values may be sent and summed in bfloat16 or wider, within the bound.
A program may use at most 128 MiB of HBM per device.

v0:
```python
import jax
import jax.numpy as jnp
from jax import lax
from jax.sharding import PartitionSpec as P

CONTRACT_LAST = (((1,), (1,)), ((), ()))
CONTRACT_FIRST = (((0,), (0,)), ((), ()))


def product(left, right, dims):
    return lax.dot_general(left, right, dims, preferred_element_type=jnp.float32)


def body(counts, mol_factor, frag_factor):
    rank_cols = mol_factor.shape[1]
    rank_rows = frag_factor.shape[0]
    frag_index = lax.axis_index("frag")
    mol_index = lax.axis_index("mol")
    columns = lax.all_gather(frag_factor, "mol", axis=0, tiled=True)
    numer_whole = product(columns, counts, CONTRACT_LAST)
    gram_whole = product(columns, columns, CONTRACT_LAST)
    numer_whole, gram_whole = lax.psum((numer_whole, gram_whole), "frag")
    numer_mine = lax.dynamic_slice_in_dim(numer_whole, frag_index * rank_cols, rank_cols, 0)
    gram_mine = lax.dynamic_slice_in_dim(gram_whole, frag_index * rank_cols, rank_cols, 0)
    gram_mine = gram_mine.astype(jnp.bfloat16)
    denom_mol = product(
        lax.all_gather(mol_factor, "frag", axis=1, tiled=True), gram_mine, CONTRACT_LAST
    )
    new_mol = (mol_factor.astype(jnp.float32) * numer_mine.T / denom_mol).astype(jnp.bfloat16)
    gathered_mol = lax.all_gather(new_mol, "frag", axis=1, tiled=True)
    numer_frag = product(gathered_mol, counts, CONTRACT_FIRST)
    gram_mol = product(gathered_mol, gathered_mol, CONTRACT_FIRST)
    numer_frag, gram_mol = lax.psum((numer_frag, gram_mol), "mol")
    numer_rows = lax.dynamic_slice_in_dim(numer_frag, mol_index * rank_rows, rank_rows, 0)
    gram_rows = lax.dynamic_slice_in_dim(gram_mol, mol_index * rank_rows, rank_rows, 0)
    denom_frag = jnp.dot(
        gram_rows.astype(jnp.bfloat16), columns, preferred_element_type=jnp.float32
    )
    new_frag = (frag_factor.astype(jnp.float32) * numer_rows / denom_frag).astype(jnp.bfloat16)
    return (new_mol, new_frag)


def solution(mesh):
    return jax.shard_map(
        body,
        mesh=mesh,
        in_specs=(P("mol", "frag"), P("mol", "frag"), P("mol", "frag")),
        out_specs=(P("mol", "frag"), P("mol", "frag")),
        check_vma=False,
    )
```

profile of v0, /device:TPU:0, one launch (start us, length us, event | category | flops | bytes accessed | tf_op | source)
XLA Modules:
  0.0 298.5 jit_solution(6649359536680511481)
XLA Ops:
  7.2 0.0 all-gather.4.cloned.1.call-start
  7.2 0.7 all-gather.4.cloned.1.call-update
  7.9 0.0 all-gather.6.cloned.1.call-start
  7.9 0.7 all-gather.6.cloned.1.call-update
  8.6 0.0 all-reduce.5.cloned.1.call-start
  8.7 31.8 %all-gather.4.cloned.1.call-done = bf16[256,4096]{1,0:T(8,128)(2,1)} async-done(((bf16[32,4096]{1,0:T(8,128)(2,1)}), bf16[256,4096]{1,0:T(8,128)(2,1)}) %all-gather.4.cloned.1.call-update) | async-done | bytes 2097168 | tf_op jit(solution)/shard_map/all_gather | solution.py:19
  40.5 12.2 %fusion.5 = f32[256,2048]{1,0:T(8,128)} fusion(bf16[256,4096]{1,0:T(8,128)(2,1)} %all-gather.4.cloned.1.call-done, bf16[2048,4096]{1,0:T(8,128)(2,1)} %param.3), kind=kOutput, calls=%fused_computation.10 | convolution fusion | flops 4294967296 | bytes 20971520 | tf_op jit(solution)/shard_map/dot_general | solution.py:11
  52.8 0.0 copy-start
  52.8 0.0 all-reduce.5.cloned.1.call-update
  52.8 0.0 all-gather.8.cloned.1.call-start
  52.8 1.5 copy-done
  54.3 0.0 copy-start.2
  54.4 0.7 fusion.6
  55.1 29.0 %all-reduce.8 = bf16[256,256]{1,0:T(8,128)(2,1)S(1)} all-reduce(f32[256,256]{1,0:T(8,128)S(1)} %fusion.6), channel_id=1, replica_groups=mesh['mol'=8,'frag'=4] {'frag'}, use_global_device_ids=true, to_apply=%region_1.0 | all-reduce | flops 65536 | bytes 393216 | tf_op jit(solution)/shard_map/psum | solution.py:22
  84.1 0.0 all-gather.6.cloned.1.call-done
  84.2 79.1 %all-reduce.5.cloned.1.call-done = f32[256,2048]{1,0:T(8,128)} async-done(((f32[256,2048]{1,0:T(8,128)}), f32[256,2048]{1,0:T(8,128)}) %all-reduce.5.cloned.1.call-update) | async-done | bytes 2097168 | tf_op jit(solution)/shard_map/psum | solution.py:22
  163.2 0.0 copy-done.2
  163.2 2.4 fusion.2
  165.6 0.0 all-gather.8.cloned.1.call-update
  165.6 0.0 all-reduce.7.cloned.1.call-start
  165.7 27.0 %all-gather.8.cloned.1.call-done = bf16[2048,256]{0,1:T(8,128)(2,1)} async-done(((bf16[2048,64]{0,1:T(8,128)(2,1)}), bf16[2048,256]{0,1:T(8,128)(2,1)}) %all-gather.8.cloned.1.call-update) | async-done | bytes 1048592 | tf_op jit(solution)/shard_map/all_gather | solution.py:30
  192.7 12.6 %fusion.7 = f32[256,4096]{1,0:T(8,128)} fusion(bf16[2048,256]{0,1:T(8,128)(2,1)} %all-gather.8.cloned.1.call-done, bf16[2048,4096]{1,0:T(8,128)(2,1)} %param.3), kind=kOutput, calls=%fused_computation.12 | convolution fusion | flops 4294967296 | bytes 22020096 | tf_op jit(solution)/shard_map/dot_general | solution.py:11
  205.3 0.0 copy-start.1
  205.3 0.0 all-reduce.7.cloned.1.call-update
  205.3 1.2 copy-done.1
  206.5 0.5 fusion.8
  207.0 31.9 %all-reduce.9 = bf16[256,256]{1,0:T(8,128)(2,1)S(1)} all-reduce(f32[256,256]{1,0:T(8,128)S(1)} %fusion.8), channel_id=1, replica_groups=mesh['mol'=8,'frag'=4] {'mol'}, use_global_device_ids=true, to_apply=%region_3.0 | all-reduce | flops 65536 | bytes 393216 | tf_op jit(solution)/shard_map/psum | solution.py:33
  238.9 50.8 %all-reduce.7.cloned.1.call-done = f32[256,4096]{1,0:T(8,128)} async-done(((f32[256,4096]{1,0:T(8,128)}), f32[256,4096]{1,0:T(8,128)}) %all-reduce.7.cloned.1.call-update) | async-done | bytes 4194320 | tf_op jit(solution)/shard_map/psum | solution.py:33
  289.7 2.3 fusion
Async XLA Ops:
  7.2 33.4 %all-gather.4.cloned.1.call-start = ((), (), s32[]{:S(2)}) async-start(), calls=%async_computation | async-start | bytes 2359296 | tf_op jit(solution)/shard_map/all_gather | solution.py:19
  7.9 76.3 %all-gather.6.cloned.1.call-start = ((), (), s32[]{:S(2)}) async-start(), calls=%async_computation.2 | async-start | bytes 1310720 | tf_op jit(solution)/shard_map/all_gather | solution.py:27
  8.6 154.6 %all-reduce.5.cloned.1.call-start = ((), (), s32[]{:S(2)}) async-start(), calls=%async_computation.1 | async-start | bytes 4194304 | tf_op jit(solution)/shard_map/psum | solution.py:22
  52.8 1.6 copy-start
  52.8 139.9 %all-gather.8.cloned.1.call-start = ((), (), s32[]{:S(2)}) async-start(), calls=%async_computation.3 | async-start | bytes 1310720 | tf_op jit(solution)/shard_map/all_gather | solution.py:30
  54.3 108.9 %copy-start.2 = (bf16[2048,64]{0,1:T(8,128)(2,1)S(1)}, bf16[2048,64]{0,1:T(8,128)(2,1)}, u32[]{:S(2)}) copy-start(bf16[2048,64]{0,1:T(8,128)(2,1)} %param.4) | copy-start | bytes 786436
  165.6 124.1 %all-reduce.7.cloned.1.call-start = ((), (), s32[]{:S(2)}) async-start(), calls=%async_computation.4 | async-start | bytes 8388608 | tf_op jit(solution)/shard_map/psum | solution.py:33
  205.3 1.2 copy-start.1
Sparse Core Ops, SparseCore 0:
  9.9 30.5 all-gather.3
  42.1 31.7 all-gather.5
  76.2 86.9 all-reduce.4
  165.8 26.8 all-gather.7
  205.4 84.2 all-reduce.6
where the time goes:
time: 299 us
  waiting for transfers between devices  190 us (64%)
  blocking collectives  61 us (20%)
  matrix products  30.7 us (10%)
  between operations  13.8 us (5%)
    psum x1, waiting for transfers between devices, body(): numer_whole, gram_whole = lax.psum((numer_whole, gram_whole), 'frag')  79.1 us
    psum x1, waiting for transfers between devices, body(): numer_frag, gram_mol = lax.psum((numer_frag, gram_mol), 'mol')  50.8 us
    psum x1, blocking collectives, body(): numer_frag, gram_mol = lax.psum((numer_frag, gram_mol), 'mol')  31.9 us
    all_gather x1, waiting for transfers between devices, body(): columns = lax.all_gather(frag_factor, 'mol', axis=0, tiled=True)  31.8 us
    psum x1, blocking collectives, body(): numer_whole, gram_whole = lax.psum((numer_whole, gram_whole), 'frag')  29 us
    dot_general x5, matrix products, product(): lax.dot_general(left, right, dims, preferred_element_type=jnp.float32)  28.4 us
    all_gather x1, waiting for transfers between devices, body(): gathered_mol = lax.all_gather(new_mol, 'frag', axis=1, tiled=True)  27 us
  transfers between devices with their start and end apart: 5, of which 4 were waited for; matrix products, arithmetic and copies ran while one was open for 5% of the time, Pallas kernels for 0%

commit v1 on v0

--- a/solution.py
+++ b/solution.py
@@ -1,6 +1,10 @@
+import functools
+
 import jax
 import jax.numpy as jnp
 from jax import lax
+from jax.experimental import pallas as pl
+from jax.experimental.pallas import tpu as pltpu
 from jax.sharding import PartitionSpec as P
 
 CONTRACT_LAST = (((1,), (1,)), ((), ()))
@@ -40,9 +44,419 @@
     return (new_mol, new_frag)
 
 
+MESH = pl.DeviceIdType.MESH
+F32 = jnp.float32
+BF16 = jnp.bfloat16
+STEPS = 4
+TILE = 1024
+PARTS = 2
+
+
+def remote(src, dst, send, recv, mol, frag):
+    return pltpu.make_async_remote_copy(
+        src_ref=src, dst_ref=dst, send_sem=send, recv_sem=recv,
+        device_id={"mol": mol, "frag": frag}, device_id_type=MESH,
+    )
+
+
+def aligned(index, size):
+    return pl.ds(pl.multiple_of(index * size, size), size)
+
+
+def kernel(
+    n_mol, n_frag, counts_hbm, w_ref, h_ref, wout, hout,
+    counts, hfull, wt, wmine, gpart, gown, gfull, acc,
+    up_out, up_in, down_out, down_in, newall, newt, psum, pin, csum, cin,
+    counts_sem, h_s, h_r, hc_s, hc_r, w_s, w_r, g_s, g_r, gp_s, gp_r,
+    up_s, up_r, down_s, down_r, ag_s, ag_r, c1_s, c1_r, c2_s, c2_r,
+):
+    chips = n_mol // 2
+    last = n_frag - 1
+    mols, cols = w_ref.shape
+    rows, frags = h_ref.shape
+    half = mols // 2
+    sub = half // STEPS
+    rank = rows * n_mol
+    m = lax.axis_index("mol")
+    z = lax.axis_index("frag")
+    chip = m // 2
+    core = m % 2
+    twin = chip * 2 + 1 - core
+    tiles = frags // TILE
+    width = frags // PARTS
+
+    load = pltpu.make_async_copy(counts_hbm, counts, counts_sem)
+    load.start()
+    hfull[aligned(m, rows), :] = h_ref[...]
+    wt[...] = w_ref[...].T
+
+    @pl.when(z == last)
+    def _():
+        wmine[aligned(z, cols), :] = wt[:, :half]
+
+    @pl.when(z == 0)
+    def _():
+        wmine[aligned(z, cols), :] = wt[:, half:]
+
+    barrier = pltpu.get_barrier_semaphore()
+    for k in range(1, n_mol):
+        pl.semaphore_signal(
+            barrier, inc=1, device_id={"mol": (m + k) % n_mol, "frag": z}, device_id_type=MESH)
+    for k in range(1, n_frag):
+        pl.semaphore_signal(
+            barrier, inc=1, device_id={"mol": m, "frag": (z + k) % n_frag}, device_id_type=MESH)
+    pl.semaphore_wait(barrier, n_mol - 1 + n_frag - 1)
+
+    def h_copy(k, p):
+        lanes = pl.ds(p * width, width)
+        return remote(
+            h_ref.at[:, lanes], hfull.at[aligned(m, rows), lanes],
+            h_s.at[k - 1, p], h_r.at[k - 1, p], ((chip + k) % chips) * 2 + core, z)
+
+    def h_twin(k, p):
+        lanes = pl.ds(p * width, width)
+        there = ((chip + chips - k) % chips) * 2 + core
+        block = hfull.at[aligned(there, rows), lanes]
+        return remote(
+            h_ref.at[:, lanes] if k == 0 else block, block,
+            hc_s.at[k, p], hc_r.at[k, p], twin, z)
+
+    for p in range(PARTS):
+        for k in range(1, chips):
+            h_copy(k, p).start()
+        h_twin(0, p).start()
+
+    to_last = remote(wt.at[:, :half], wmine.at[aligned(z, cols), :], w_s.at[0], w_r.at[z], m, last)
+    to_first = remote(wt.at[:, half:], wmine.at[aligned(z, cols), :], w_s.at[1], w_r.at[z], m, 0)
+
+    @pl.when(z < last)
+    def _():
+        to_last.start()
+
+    @pl.when(z > 0)
+    def _():
+        to_first.start()
+
+    for p in range(PARTS):
+        for k in range(1, chips):
+            h_copy(k, p).wait_recv()
+            h_twin(k, p).start()
+    for p in range(PARTS):
+        for k in range(chips):
+            h_twin(k, p).wait_recv()
+
+    gown[...] = product(h_ref[...], hfull[...], CONTRACT_LAST)
+    g_last = remote(gown, gpart.at[z], g_s.at[0], g_r.at[z], m, last)
+    g_first = remote(gown, gpart.at[z], g_s.at[1], g_r.at[z], m, 0)
+
+    @pl.when(z < last)
+    def _():
+        g_last.start()
+
+    @pl.when(z > 0)
+    def _():
+        g_first.start()
+
+    load.wait()
+
+    def g_share(k):
+        block = gfull.at[aligned(m, rows), :]
+        return remote(block, block, gp_s.at[k - 1], gp_r.at[k - 1], (m + k) % n_mol, z)
+
+    def owner_ready():
+        total = gown[...]
+        for k in range(1, n_frag):
+            there = (z + k) % n_frag
+            remote(gown, gpart.at[there], g_s.at[0], g_r.at[there], m, z).wait_recv()
+            total = total + gpart[there]
+        gfull[aligned(m, rows), :] = total.astype(BF16)
+        for k in range(1, n_mol):
+            g_share(k).start()
+        for k in range(1, n_frag):
+            there = (z + k) % n_frag
+            remote(wt.at[:, :half], wmine.at[aligned(there, cols), :], w_s.at[0], w_r.at[there], m, z).wait_recv()
+        for k in range(1, n_mol):
+            g_share(k).wait_recv()
+
+    def ag_copy(side, s):
+        block = newall.at[aligned(s + side * STEPS, sub), :]
+        return remote(
+            block, block, ag_s.at[side, s], ag_r.at[side, s], m, z - 1 if side == 0 else z + 1)
+
+    def arrived(side, s):
+        here = aligned(s + side * STEPS, sub)
+        newt[:, here] = newall[here, :].T
+
+    def reduce_step(side, s, outs, ins, send, recv):
+        here = aligned(s + side * STEPS, sub)
+        acc[...] = product(counts[here, :], hfull[...], CONTRACT_LAST)
+        first, end = (0, last) if side == 0 else (last, 0)
+        onward = remote(outs.at[s], ins.at[s], send.at[s], recv.at[s], m, z + 1 if side == 0 else z - 1)
+
+        @pl.when(z != first)
+        def _():
+            onward.wait_recv()
+            acc[...] += ins[s].astype(F32)
+
+        @pl.when(z != end)
+        def _():
+            outs[s] = acc[...].astype(BF16)
+            onward.start()
+
+        @pl.when(z == end)
+        def _():
+            w = wmine[:, aligned(s, sub)].T
+            denom = product(w, gfull[...], (((1,), (0,)), ((), ())))
+            newall[here, :] = (w.astype(F32) * acc[...] / denom).astype(BF16)
+            ag_copy(side, s).start()
+            arrived(side, s)
+
+    def gather_step(side, s):
+        ag_copy(side, s).wait_recv()
+
+        @pl.when(z != (0 if side == 0 else last))
+        def _():
+            ag_copy(side, s).start()
+
+        arrived(side, s)
+
+    def within(s):
+        return jnp.logical_and(s >= 0, s < STEPS)
+
+    def tick(t, carry):
+        @pl.when(jnp.logical_and(t == last, jnp.logical_or(z == 0, z == last)))
+        def _():
+            owner_ready()
+
+        up = t - z
+        down = t - (last - z)
+        from_last = t - last - (last - z)
+        from_first = t - last - z
+
+        @pl.when(within(up))
+        def _():
+            reduce_step(0, up, up_out, up_in, up_s, up_r)
+
+        @pl.when(within(down))
+        def _():
+            reduce_step(1, down, down_out, down_in, down_s, down_r)
+
+        @pl.when(jnp.logical_and(within(from_last), z < last))
+        def _():
+            gather_step(0, from_last)
+
+        @pl.when(jnp.logical_and(within(from_first), z > 0))
+        def _():
+            gather_step(1, from_first)
+
+        return carry
+
+    lax.fori_loop(0, STEPS + 2 * last, tick, 0)
+
+    def twin_copy(q, lanes):
+        return remote(
+            psum.at[:, 1 - core, :, lanes], pin.at[:, :, lanes], c1_s.at[q], c1_r.at[q], twin, z)
+
+    def chip_copy(k, q, lanes):
+        there = (chip + k) % chips
+        return remote(
+            csum.at[there, :, lanes], cin.at[k - 1, :, lanes],
+            c2_s.at[k - 1, q], c2_r.at[k - 1, q], there * 2 + core, z)
+
+    def send_twin(q, lanes, part):
+        psum[:, :, :, lanes] = part.astype(BF16).reshape(chips, 2, rows, part.shape[1])
+        twin_copy(q, lanes).start()
+
+    def send_chips(q, lanes):
+        twin_copy(q, lanes).wait_recv()
+        both = psum[:, core, :, lanes].astype(F32) + pin[:, :, lanes].astype(F32)
+        csum[:, :, lanes] = both.astype(BF16)
+        for k in range(1, chips):
+            chip_copy(k, q, lanes).start()
+
+    def total(q, lanes):
+        for k in range(1, chips):
+            chip_copy(k, q, lanes).wait_recv()
+        value = psum[chip, core, :, lanes].astype(F32) + pin[chip, :, lanes].astype(F32)
+        for k in range(1, chips):
+            value = value + cin[k - 1, :, lanes].astype(F32)
+        return value
+
+    gram_lanes = pl.ds(frags, rank)
+    plain = (((1,), (0,)), ((), ()))
+    send_twin(tiles, gram_lanes, product(newt[...], newall[...], plain))
+
+    def second(q, carry):
+        lanes = aligned(q, TILE)
+        send_twin(q, lanes, product(newt[...], counts[:, lanes], plain))
+
+        @pl.when(q == 0)
+        def _():
+            send_chips(tiles, gram_lanes)
+
+        @pl.when(q > 0)
+        def _():
+            send_chips(q - 1, aligned(q - 1, TILE))
+
+        return carry
+
+    lax.fori_loop(0, tiles, second, 0)
+    send_chips(tiles - 1, pl.ds((tiles - 1) * TILE, TILE))
+
+    for k in range(n_frag):
+        @pl.when(z == k)
+        def _(k=k):
+            wout[...] = newall[:, k * cols:(k + 1) * cols]
+
+    @pl.when(z < last)
+    def _():
+        g_last.wait_send()
+
+    @pl.when(z > 0)
+    def _():
+        g_first.wait_send()
+
+    gram = total(tiles, gram_lanes).astype(BF16)
+    gown[...] = gram.astype(F32)
+
+    def finish(q, carry):
+        lanes = aligned(q, TILE)
+        denom = product(gown[...].astype(BF16), hfull[:, lanes], plain)
+        hout[:, lanes] = (h_ref[:, lanes].astype(F32) * total(q, lanes) / denom).astype(BF16)
+        return carry
+
+    lax.fori_loop(0, tiles, finish, 0)
+
+    for p in range(PARTS):
+        for k in range(1, chips):
+            h_copy(k, p).wait_send()
+        for k in range(chips):
+            h_twin(k, p).wait_send()
+
+    @pl.when(z < last)
+    def _():
+        to_last.wait_send()
+
+    @pl.when(z > 0)
+    def _():
+        to_first.wait_send()
+
+    @pl.when(jnp.logical_or(z == 0, z == last))
+    def _():
+        for k in range(1, n_mol):
+            g_share(k).wait_send()
+
+    def drain(s, carry):
+        @pl.when(z < last)
+        def _():
+            remote(up_out.at[s], up_in.at[s], up_s.at[s], up_r.at[s], m, z + 1).wait_send()
+            ag_copy(1, s).wait_send()
+
+        @pl.when(z > 0)
+        def _():
+            remote(down_out.at[s], down_in.at[s], down_s.at[s], down_r.at[s], m, z - 1).wait_send()
+            ag_copy(0, s).wait_send()
+
+        return carry
+
+    lax.fori_loop(0, STEPS, drain, 0)
+
+    def drain_tile(q, carry):
+        lanes = aligned(q, TILE)
+        twin_copy(q, lanes).wait_send()
+        for k in range(1, chips):
+            chip_copy(k, q, lanes).wait_send()
+        return carry
+
+    lax.fori_loop(0, tiles, drain_tile, 0)
+    twin_copy(tiles, gram_lanes).wait_send()
+    for k in range(1, chips):
+        chip_copy(k, tiles, gram_lanes).wait_send()
+
+
+def fused(n_mol, n_frag, counts, mol_factor, frag_factor):
+    mols, cols = mol_factor.shape
+    rows, frags = frag_factor.shape
+    rank = rows * n_mol
+    chips = n_mol // 2
+    half = mols // 2
+    sub = half // STEPS
+    tiles = frags // TILE
+    dma = pltpu.SemaphoreType.DMA
+    vmem = pltpu.VMEM
+    scratch = [
+        vmem((mols, frags), BF16),
+        vmem((rank, frags), BF16),
+        vmem((cols, mols), BF16),
+        vmem((rank, half), BF16),
+        vmem((n_frag, rows, rank), F32),
+        vmem((rows, rank), F32),
+        vmem((rank, rank), BF16),
+        vmem((sub, rank), F32),
+        vmem((STEPS, sub, rank), BF16),
+        vmem((STEPS, sub, rank), BF16),
+        vmem((STEPS, sub, rank), BF16),
+        vmem((STEPS, sub, rank), BF16),
+        vmem((mols, rank), BF16),
+        vmem((rank, mols), BF16),
+        vmem((chips, 2, rows, frags + rank), BF16),
+        vmem((chips, rows, frags + rank), BF16),
+        vmem((chips, rows, frags + rank), BF16),
+        vmem((chips - 1, rows, frags + rank), BF16),
+        dma,
+        dma((chips - 1, PARTS)), dma((chips - 1, PARTS)),
+        dma((chips, PARTS)), dma((chips, PARTS)),
+        dma((2,)), dma((n_frag,)),
+        dma((2,)), dma((n_frag,)),
+        dma((n_mol - 1,)), dma((n_mol - 1,)),
+        dma((STEPS,)), dma((STEPS,)), dma((STEPS,)), dma((STEPS,)),
+        dma((2, STEPS)), dma((2, STEPS)),
+        dma((tiles + 1,)), dma((tiles + 1,)),
+        dma((chips - 1, tiles + 1)), dma((chips - 1, tiles + 1)),
+    ]
+    return pl.pallas_call(
+        functools.partial(kernel, n_mol, n_frag),
+        out_shape=(
+            jax.ShapeDtypeStruct((mols, cols), BF16),
+            jax.ShapeDtypeStruct((rows, frags), BF16),
+        ),
+        in_specs=[
+            pl.BlockSpec(memory_space=pl.ANY),
+            pl.BlockSpec(memory_space=pltpu.VMEM),
+            pl.BlockSpec(memory_space=pltpu.VMEM),
+        ],
+        out_specs=(
+            pl.BlockSpec(memory_space=pltpu.VMEM),
+            pl.BlockSpec(memory_space=pltpu.VMEM),
+        ),
+        scratch_shapes=scratch,
+        compiler_params=pltpu.CompilerParams(
+            collective_id=0, has_side_effects=True, vmem_limit_bytes=56 * 1024 * 1024
+        ),
+        cost_estimate=pl.CostEstimate(
+            flops=4 * mols * frags * rank, bytes_accessed=2 * mols * frags, transcendentals=0
+        ),
+    )(counts, mol_factor, frag_factor)
+
+
+def fits(n_mol, n_frag, mols, cols, rows, frags):
+    return (
+        n_mol % 2 == 0 and n_mol > 2 and n_frag > 1 and rows % 16 == 0 and cols % 16 == 0
+        and mols % (2 * STEPS * 128) == 0 and frags % (TILE * PARTS) == 0
+        and (rows * n_mol) % 128 == 0 and mols * frags <= 2 ** 23 and n_mol <= 8
+    )
+
+
 def solution(mesh):
+    n_mol, n_frag = mesh.shape["mol"], mesh.shape["frag"]
+
+    def local(counts, mol_factor, frag_factor):
+        if fits(n_mol, n_frag, *mol_factor.shape, *frag_factor.shape):
+            return fused(n_mol, n_frag, counts, mol_factor, frag_factor)
+        return body(counts, mol_factor, frag_factor)
+
     return jax.shard_map(
-        body,
+        local,
         mesh=mesh,
         in_specs=(P("mol", "frag"), P("mol", "frag"), P("mol", "frag")),
         out_specs=(P("mol", "frag"), P("mol", "frag")),

time: 299 us -> 92.2 us (0.31)
  waiting for transfers between devices: 190 us -> 0 us
  Pallas kernels: 0 us -> 85.8 us
  blocking collectives: 61 us -> 0 us
  matrix products: 30.7 us -> 0 us
  between operations: 13.8 us -> 0.64 us
    psum x2 -> x0, waiting for transfers between devices: 130 us -> none  [the longest x1 79.1 us: body(): numer_whole, gram_whole = lax.psum((numer_whole, gram_whole), 'frag')]
    pallas_call x0 -> x1, Pallas kernels: none -> 85.8 us  [fused(): pl.pallas_call(functools.partial(kernel, n_mol, n_frag), out_shape=(jax.S...]
    psum x2 -> x0, blocking collectives: 61 us -> none  [the longest x1 31.9 us: body(): numer_frag, gram_mol = lax.psum((numer_frag, gram_mol), 'mol')]
    all_gather x3 -> x0, waiting for transfers between devices: 58.8 us -> none  [the longest x1 31.8 us: body(): columns = lax.all_gather(frag_factor, 'mol', axis=0, tiled=True)]
    dot_general x6 -> x0, matrix products: 30.7 us -> none  [the longest x5 28.4 us: product(): lax.dot_general(left, right, dims, preferred_element_type=jnp.float32)]
  transfers between devices with their start and end apart: 5 -> 0, of which waited for: 4 -> 0; matrix products, arithmetic and copies ran while one was open for 5% -> 0% of each run, Pallas kernels for 0% -> 0%
where the time goes in v1:
time: 92.2 us; the launch traced here: 92 us
  Pallas kernels  85.8 us (93%)
  local copies, waits for them, and re-layouts  5.55 us (6%)
    pallas_call x1, Pallas kernels, fused(): pl.pallas_call(functools.partial(kernel, n_mol, n_frag), out_shape=(jax.S...  85.8 us
    unnamed x2, local copies, waits for them, and re-layouts  3.61 us
    pallas_call x1, local copies, waits for them, and re-layouts, fused(): pl.pallas_call(functools.partial(kernel, n_mol, n_frag), out_shape=(jax.S...  1.93 us

profile of v1, /device:TPU:0, one launch (start us, length us, event | category | flops | bytes accessed | tf_op | source)
XLA Modules:
  0.0 92.0 jit_solution(3818180024735797868)
XLA Ops:
  0.6 1.9 %copy.5.w_ref = bf16[2048,64]{1,0:T(8,128)(2,1)} copy(bf16[2048,64]{0,1:T(8,128)(2,1)} %param.4) | data formatting | bytes 524288 | tf_op args[1]
  2.6 85.8 %shard_map.50 = (bf16[2048,64]{1,0:T(8,128)(2,1)}, bf16[32,4096]{1,0:T(8,128)(2,1)}) custom-call(bf16[2048,4096]{1,0:T(8,128)(2,1)} %counts_hbm.1, bf16[2048,64]{1,0:T(8,128)(2,1)} %copy.5.w_ref, bf16[32,4096]{1,0:T(8,128)(2,1)} %h_ref.1), custom_call_target="tpu_custom_call" | custom-call | flops 8589934592 | bytes 16777216 | tf_op jit(solution)/shard_map/pallas_call | solution.py:417
  88.4 1.9 %copy.6 = bf16[2048,64]{0,1:T(8,128)(2,1)} copy(bf16[2048,64]{1,0:T(8,128)(2,1)} %get-tuple-element.2) | data formatting | bytes 524288 | tf_op jit(solution)/shard_map/pallas_call | solution.py:417
  90.3 1.7 %copy.8 = bf16[32,4096]{1,0:T(8,128)(2,1)} copy(bf16[32,4096]{1,0:T(8,128)(2,1)} %get-tuple-element.7) | data formatting | bytes 524288

commit v2 on v1

--- a/solution.py
+++ b/solution.py
@@ -47,8 +47,11 @@
 MESH = pl.DeviceIdType.MESH
 F32 = jnp.float32
 BF16 = jnp.bfloat16
-STEPS = 4
-TILE = 1024
+PLAIN = (((1,), (0,)), ((), ()))
+STEPS = 16
+GROUP = 2
+LAG = 2
+TILE = 512
 PARTS = 2
 
 
@@ -64,39 +67,38 @@
 
 
 def kernel(
-    n_mol, n_frag, counts_hbm, w_ref, h_ref, wout, hout,
-    counts, hfull, wt, wmine, gpart, gown, gfull, acc,
-    up_out, up_in, down_out, down_in, newall, newt, psum, pin, csum, cin,
+    n_mol, n_frag, counts_hbm, wt, h_ref, wout, hout,
+    counts, hfull, wmine, gpart, gown, gfull, mine,
+    edge_out, edge_in, mid_out, mid_in, newall, newt, ahead_sum, psum, pin, csum, cin,
     counts_sem, h_s, h_r, hc_s, hc_r, w_s, w_r, g_s, g_r, gp_s, gp_r,
-    up_s, up_r, down_s, down_r, ag_s, ag_r, c1_s, c1_r, c2_s, c2_r,
+    edge_s, edge_r, mid_s, mid_r, ag_s, ag_r, c1_s, c1_r, c2_s, c2_r,
 ):
     chips = n_mol // 2
-    last = n_frag - 1
-    mols, cols = w_ref.shape
+    cols, mols = wt.shape
     rows, frags = h_ref.shape
     half = mols // 2
-    sub = half // STEPS
+    sub = mols // STEPS
     rank = rows * n_mol
+    block = 2 * frags // STEPS
     m = lax.axis_index("mol")
     z = lax.axis_index("frag")
     chip = m // 2
     core = m % 2
     twin = chip * 2 + 1 - core
+    inner = jnp.logical_or(z == 1, z == 2)
+    outer = jnp.logical_not(inner)
+    pair = z + 1 - 2 * (z % 2)
+    across = 3 - z
     tiles = frags // TILE
     width = frags // PARTS
 
     load = pltpu.make_async_copy(counts_hbm, counts, counts_sem)
     load.start()
     hfull[aligned(m, rows), :] = h_ref[...]
-    wt[...] = w_ref[...].T
-
-    @pl.when(z == last)
+
+    @pl.when(inner)
     def _():
-        wmine[aligned(z, cols), :] = wt[:, :half]
-
-    @pl.when(z == 0)
-    def _():
-        wmine[aligned(z, cols), :] = wt[:, half:]
+        wmine[aligned(z, cols), :] = wt[...]
 
     barrier = pltpu.get_barrier_semaphore()
     for k in range(1, n_mol):
@@ -126,16 +128,13 @@
             h_copy(k, p).start()
         h_twin(0, p).start()
 
-    to_last = remote(wt.at[:, :half], wmine.at[aligned(z, cols), :], w_s.at[0], w_r.at[z], m, last)
-    to_first = remote(wt.at[:, half:], wmine.at[aligned(z, cols), :], w_s.at[1], w_r.at[z], m, 0)
-
-    @pl.when(z < last)
-    def _():
-        to_last.start()
-
-    @pl.when(z > 0)
-    def _():
-        to_first.start()
+    w_copies = [
+        remote(wt, wmine.at[aligned(z, cols), :], w_s.at[e], w_r.at[z], m, e + 1) for e in range(2)
+    ]
+    for e in range(2):
+        @pl.when(z != e + 1)
+        def _(e=e):
+            w_copies[e].start()
 
     for p in range(PARTS):
         for k in range(1, chips):
@@ -145,17 +144,13 @@
         for k in range(chips):
             h_twin(k, p).wait_recv()
 
-    gown[...] = product(h_ref[...], hfull[...], CONTRACT_LAST)
-    g_last = remote(gown, gpart.at[z], g_s.at[0], g_r.at[z], m, last)
-    g_first = remote(gown, gpart.at[z], g_s.at[1], g_r.at[z], m, 0)
-
-    @pl.when(z < last)
-    def _():
-        g_last.start()
-
-    @pl.when(z > 0)
-    def _():
-        g_first.start()
+    g_copies = [remote(gown, gpart.at[z], g_s.at[e], g_r.at[z], m, e + 1) for e in range(2)]
+    def share_gram():
+        gown[...] = product(h_ref[...], hfull[...], CONTRACT_LAST)
+        for e in range(2):
+            @pl.when(z != e + 1)
+            def _(e=e):
+                g_copies[e].start()
 
     load.wait()
 
@@ -174,84 +169,91 @@
             g_share(k).start()
         for k in range(1, n_frag):
             there = (z + k) % n_frag
-            remote(wt.at[:, :half], wmine.at[aligned(there, cols), :], w_s.at[0], w_r.at[there], m, z).wait_recv()
+            remote(wt, wmine.at[aligned(there, cols), :], w_s.at[0], w_r.at[there], m, z).wait_recv()
         for k in range(1, n_mol):
             g_share(k).wait_recv()
 
-    def ag_copy(side, s):
-        block = newall.at[aligned(s + side * STEPS, sub), :]
-        return remote(
-            block, block, ag_s.at[side, s], ag_r.at[side, s], m, z - 1 if side == 0 else z + 1)
-
-    def arrived(side, s):
-        here = aligned(s + side * STEPS, sub)
+    def edge_copy(s):
+        return remote(edge_out.at[s], edge_in.at[s], edge_s.at[s], edge_r.at[s], m, pair)
+
+    def mid_copy(s):
+        return remote(mid_out.at[s], mid_in.at[s], mid_s.at[s], mid_r.at[s], m, across)
+
+    def ag_copy(s):
+        part = newall.at[aligned(s, sub), :]
+        return remote(part, part, ag_s.at[s], ag_r.at[s], m, pair)
+
+    def arrived(s):
+        here = aligned(s, sub)
         newt[:, here] = newall[here, :].T
 
-    def reduce_step(side, s, outs, ins, send, recv):
-        here = aligned(s + side * STEPS, sub)
-        acc[...] = product(counts[here, :], hfull[...], CONTRACT_LAST)
-        first, end = (0, last) if side == 0 else (last, 0)
-        onward = remote(outs.at[s], ins.at[s], send.at[s], recv.at[s], m, z + 1 if side == 0 else z - 1)
-
-        @pl.when(z != first)
-        def _():
-            onward.wait_recv()
-            acc[...] += ins[s].astype(F32)
-
-        @pl.when(z != end)
-        def _():
-            outs[s] = acc[...].astype(BF16)
-            onward.start()
-
-        @pl.when(z == end)
-        def _():
-            w = wmine[:, aligned(s, sub)].T
-            denom = product(w, gfull[...], (((1,), (0,)), ((), ())))
-            newall[here, :] = (w.astype(F32) * acc[...] / denom).astype(BF16)
-            ag_copy(side, s).start()
-            arrived(side, s)
-
-    def gather_step(side, s):
-        ag_copy(side, s).wait_recv()
-
-        @pl.when(z != (0 if side == 0 else last))
-        def _():
-            ag_copy(side, s).start()
-
-        arrived(side, s)
-
-    def within(s):
-        return jnp.logical_and(s >= 0, s < STEPS)
-
-    def tick(t, carry):
-        @pl.when(jnp.logical_and(t == last, jnp.logical_or(z == 0, z == last)))
-        def _():
-            owner_ready()
-
-        up = t - z
-        down = t - (last - z)
-        from_last = t - last - (last - z)
-        from_first = t - last - z
-
-        @pl.when(within(up))
-        def _():
-            reduce_step(0, up, up_out, up_in, up_s, up_r)
-
-        @pl.when(within(down))
-        def _():
-            reduce_step(1, down, down_out, down_in, down_s, down_r)
-
-        @pl.when(jnp.logical_and(within(from_last), z < last))
-        def _():
-            gather_step(0, from_last)
-
-        @pl.when(jnp.logical_and(within(from_first), z > 0))
-        def _():
-            gather_step(1, from_first)
-
-        return carry
-
-    lax.fori_loop(0, STEPS + 2 * last, tick, 0)
+        @pl.when(s >= STEPS // 2)
+        def _():
+            lanes = aligned(s - STEPS // 2, block)
+            ahead_sum[:, lanes] = product(newt[:, :half], counts[:half, lanes], PLAIN)
+
+    def partial_sum(s):
+        @pl.when(s % GROUP == 0)
+        def _():
+            rows_of = aligned(s // GROUP, GROUP * sub)
+            mine[...] = product(counts[rows_of, :], hfull[...], CONTRACT_LAST)
+
+        return mine[aligned(s % GROUP, sub), :]
+
+    @pl.when(outer)
+    def _():
+        def send(s, carry):
+            edge_out[s] = partial_sum(s).astype(BF16)
+            edge_copy(s).start()
+
+            @pl.when(s == GROUP - 1)
+            def _():
+                share_gram()
+
+            return carry
+
+        def take(s, carry):
+            ag_copy(s).wait_recv()
+            arrived(s)
+            return carry
+
+        lax.fori_loop(0, STEPS, send, 0)
+        lax.fori_loop(0, STEPS, take, 0)
+
+    @pl.when(inner)
+    def _():
+        def step(i, carry):
+            @pl.when(i < STEPS)
+            def _():
+                here_sum = partial_sum(i)
+
+                @pl.when(i == 0)
+                def _():
+                    share_gram()
+
+                edge_copy(i).wait_recv()
+                mid_out[i] = (here_sum + edge_in[i].astype(F32)).astype(BF16)
+                mid_copy(i).start()
+
+            @pl.when(i == LAG)
+            def _():
+                owner_ready()
+
+            @pl.when(i >= LAG)
+            def _():
+                s = i - LAG
+                here = aligned(s, sub)
+                mid_copy(s).wait_recv()
+                numer = mid_out[s].astype(F32) + mid_in[s].astype(F32)
+                w = wmine[:, here].T
+                denom = product(w, gfull[...], PLAIN)
+                newall[here, :] = (w.astype(F32) * numer / denom).astype(BF16)
+                ag_copy(s).start()
+                arrived(s)
+
+            return carry
+
+        lax.fori_loop(0, STEPS + LAG, step, 0)
 
     def twin_copy(q, lanes):
         return remote(
@@ -283,12 +285,12 @@
         return value
 
     gram_lanes = pl.ds(frags, rank)
-    plain = (((1,), (0,)), ((), ()))
-    send_twin(tiles, gram_lanes, product(newt[...], newall[...], plain))
+    send_twin(tiles, gram_lanes, product(newt[...], newall[...], PLAIN))
 
     def second(q, carry):
         lanes = aligned(q, TILE)
-        send_twin(q, lanes, product(newt[...], counts[:, lanes], plain))
+        rest = product(newt[:, half:], counts[half:, lanes], PLAIN)
+        send_twin(q, lanes, ahead_sum[:, lanes] + rest)
 
         @pl.when(q == 0)
         def _():
@@ -303,25 +305,19 @@
     lax.fori_loop(0, tiles, second, 0)
     send_chips(tiles - 1, pl.ds((tiles - 1) * TILE, TILE))
 
-    for k in range(n_frag):
-        @pl.when(z == k)
-        def _(k=k):
-            wout[...] = newall[:, k * cols:(k + 1) * cols]
-
-    @pl.when(z < last)
-    def _():
-        g_last.wait_send()
-
-    @pl.when(z > 0)
-    def _():
-        g_first.wait_send()
+    wout[...] = newt[aligned(z, cols), :]
+
+    for e in range(2):
+        @pl.when(z != e + 1)
+        def _(e=e):
+            g_copies[e].wait_send()
 
     gram = total(tiles, gram_lanes).astype(BF16)
     gown[...] = gram.astype(F32)
 
     def finish(q, carry):
         lanes = aligned(q, TILE)
-        denom = product(gown[...].astype(BF16), hfull[:, lanes], plain)
+        denom = product(gown[...].astype(BF16), hfull[:, lanes], PLAIN)
         hout[:, lanes] = (h_ref[:, lanes].astype(F32) * total(q, lanes) / denom).astype(BF16)
         return carry
 
@@ -333,29 +329,25 @@
         for k in range(chips):
             h_twin(k, p).wait_send()
 
-    @pl.when(z < last)
-    def _():
-        to_last.wait_send()
-
-    @pl.when(z > 0)
-    def _():
-        to_first.wait_send()
-
-    @pl.when(jnp.logical_or(z == 0, z == last))
+    for e in range(2):
+        @pl.when(z != e + 1)
+        def _(e=e):
+            w_copies[e].wait_send()
+
+    @pl.when(inner)
     def _():
         for k in range(1, n_mol):
             g_share(k).wait_send()
 
     def drain(s, carry):
-        @pl.when(z < last)
-        def _():
-            remote(up_out.at[s], up_in.at[s], up_s.at[s], up_r.at[s], m, z + 1).wait_send()
-            ag_copy(1, s).wait_send()
-
-        @pl.when(z > 0)
-        def _():
-            remote(down_out.at[s], down_in.at[s], down_s.at[s], down_r.at[s], m, z - 1).wait_send()
-            ag_copy(0, s).wait_send()
+        @pl.when(outer)
+        def _():
+            edge_copy(s).wait_send()
+
+        @pl.when(inner)
+        def _():
+            mid_copy(s).wait_send()
+            ag_copy(s).wait_send()
 
         return carry
 
@@ -379,26 +371,25 @@
     rows, frags = frag_factor.shape
     rank = rows * n_mol
     chips = n_mol // 2
-    half = mols // 2
-    sub = half // STEPS
+    sub = mols // STEPS
     tiles = frags // TILE
     dma = pltpu.SemaphoreType.DMA
     vmem = pltpu.VMEM
     scratch = [
         vmem((mols, frags), BF16),
         vmem((rank, frags), BF16),
-        vmem((cols, mols), BF16),
-        vmem((rank, half), BF16),
+        vmem((rank, mols), BF16),
         vmem((n_frag, rows, rank), F32),
         vmem((rows, rank), F32),
         vmem((rank, rank), BF16),
-        vmem((sub, rank), F32),
+        vmem((GROUP * sub, rank), F32),
         vmem((STEPS, sub, rank), BF16),
         vmem((STEPS, sub, rank), BF16),
         vmem((STEPS, sub, rank), BF16),
         vmem((STEPS, sub, rank), BF16),
         vmem((mols, rank), BF16),
         vmem((rank, mols), BF16),
+        vmem((rank, frags), F32),
         vmem((chips, 2, rows, frags + rank), BF16),
         vmem((chips, rows, frags + rank), BF16),
         vmem((chips, rows, frags + rank), BF16),
@@ -410,14 +401,14 @@
         dma((2,)), dma((n_frag,)),
         dma((n_mol - 1,)), dma((n_mol - 1,)),
         dma((STEPS,)), dma((STEPS,)), dma((STEPS,)), dma((STEPS,)),
-        dma((2, STEPS)), dma((2, STEPS)),
+        dma((STEPS,)), dma((STEPS,)),
         dma((tiles + 1,)), dma((tiles + 1,)),
         dma((chips - 1, tiles + 1)), dma((chips - 1, tiles + 1)),
     ]
-    return pl.pallas_call(
+    new_mol, new_frag = pl.pallas_call(
         functools.partial(kernel, n_mol, n_frag),
         out_shape=(
-            jax.ShapeDtypeStruct((mols, cols), BF16),
+            jax.ShapeDtypeStruct((cols, mols), BF16),
             jax.ShapeDtypeStruct((rows, frags), BF16),
         ),
         in_specs=[
@@ -436,13 +427,14 @@
         cost_estimate=pl.CostEstimate(
             flops=4 * mols * frags * rank, bytes_accessed=2 * mols * frags, transcendentals=0
         ),
-    )(counts, mol_factor, frag_factor)
+    )(counts, mol_factor.T, frag_factor)
+    return new_mol.T, new_frag
 
 
 def fits(n_mol, n_frag, mols, cols, rows, frags):
     return (
-        n_mol % 2 == 0 and n_mol > 2 and n_frag > 1 and rows % 16 == 0 and cols % 16 == 0
-        and mols % (2 * STEPS * 128) == 0 and frags % (TILE * PARTS) == 0
+        n_mol % 2 == 0 and n_mol > 2 and n_frag == 4 and rows % 16 == 0 and cols % 16 == 0
+        and mols % (STEPS * 128) == 0 and frags % (TILE * PARTS * 2) == 0
         and (rows * n_mol) % 128 == 0 and mols * frags <= 2 ** 23 and n_mol <= 8
     )
 

time: 92.2 us -> 81.6 us (0.89)
  Pallas kernels: 85.8 us -> 77.4 us
  local copies, waits for them, and re-layouts: 5.55 us -> 3.34 us
    pallas_call x1, Pallas kernels: 85.8 us -> 77.4 us  [fused(): pl.pallas_call(functools.partial(kernel, n_mol, n_frag), out_shape=(jax.S...]
    pallas_call x1 -> x0, local copies, waits for them, and re-layouts: 1.93 us -> none  [fused(): pl.pallas_call(functools.partial(kernel, n_mol, n_frag), out_shape=(jax.S...]
where the time goes in v2:
time: 81.6 us; the launch traced here: 81.4 us
  Pallas kernels  77.4 us (95%)
  local copies, waits for them, and re-layouts  3.34 us (4%)
    pallas_call x1, Pallas kernels, fused(): pl.pallas_call(functools.partial(kernel, n_mol, n_frag), out_shape=(jax.S...  77.4 us
    unnamed x2, local copies, waits for them, and re-layouts  3.34 us

profile of v2, /device:TPU:0, one launch (start us, length us, event | category | flops | bytes accessed | tf_op | source)
XLA Modules:
  0.0 81.4 jit_solution(1454453700254326459)
XLA Ops:
  0.6 77.4 %shard_map.50 = (bf16[64,2048]{1,0:T(8,128)(2,1)}, bf16[32,4096]{1,0:T(8,128)(2,1)}) custom-call(bf16[2048,4096]{1,0:T(8,128)(2,1)} %counts_hbm.1, bf16[64,2048]{1,0:T(8,128)(2,1)} %bitcast.3, bf16[32,4096]{1,0:T(8,128)(2,1)} %h_ref.1), custom_call_target="tpu_custom_call" | custom-call | flops 8589934592 | bytes 16777216 | tf_op jit(solution)/shard_map/pallas_call | solution.py:408
  78.0 1.7 %copy.7 = bf16[2048,64]{0,1:T(8,128)(2,1)} copy(bf16[2048,64]{0,1:T(8,128)(2,1)} %bitcast.2) | data formatting | bytes 524288
  79.7 1.7 %copy.8 = bf16[32,4096]{1,0:T(8,128)(2,1)} copy(bf16[32,4096]{1,0:T(8,128)(2,1)} %get-tuple-element.9) | data formatting | bytes 524288

commit v3 on v2

--- a/solution.py
+++ b/solution.py
@@ -167,6 +167,8 @@
         gfull[aligned(m, rows), :] = total.astype(BF16)
         for k in range(1, n_mol):
             g_share(k).start()
+
+    def owner_complete():
         for k in range(1, n_frag):
             there = (z + k) % n_frag
             remote(wt, wmine.at[aligned(there, cols), :], w_s.at[0], w_r.at[there], m, z).wait_recv()
@@ -235,9 +237,13 @@
                 mid_out[i] = (here_sum + edge_in[i].astype(F32)).astype(BF16)
                 mid_copy(i).start()
 
+            @pl.when(i == LAG - 1)
+            def _():
+                owner_ready()
+
             @pl.when(i == LAG)
             def _():
-                owner_ready()
+                owner_complete()
 
             @pl.when(i >= LAG)
             def _():

time: 81.6 us -> 80.2 us (0.983)
  Pallas kernels: 77.4 us -> 76 us
    pallas_call x1, Pallas kernels: 77.4 us -> 76 us  [fused(): pl.pallas_call(functools.partial(kernel, n_mol, n_frag), out_shape=(jax.S...]
where the time goes in v3:
time: 80.2 us; the launch traced here: 80 us
  Pallas kernels  76 us (95%)
  local copies, waits for them, and re-layouts  3.34 us (4%)
    pallas_call x1, Pallas kernels, fused(): pl.pallas_call(functools.partial(kernel, n_mol, n_frag), out_shape=(jax.S...  76 us
    unnamed x2, local copies, waits for them, and re-layouts  3.34 us

profile of v3, /device:TPU:0, one launch (start us, length us, event | category | flops | bytes accessed | tf_op | source)
XLA Modules:
  0.0 80.0 jit_solution(7650194836168380540)
XLA Ops:
  0.6 76.0 %shard_map.50 = (bf16[64,2048]{1,0:T(8,128)(2,1)}, bf16[32,4096]{1,0:T(8,128)(2,1)}) custom-call(bf16[2048,4096]{1,0:T(8,128)(2,1)} %counts_hbm.1, bf16[64,2048]{1,0:T(8,128)(2,1)} %bitcast.3, bf16[32,4096]{1,0:T(8,128)(2,1)} %h_ref.1), custom_call_target="tpu_custom_call" | custom-call | flops 8589934592 | bytes 16777216 | tf_op jit(solution)/shard_map/pallas_call | solution.py:414
  76.7 1.7 %copy.7 = bf16[2048,64]{0,1:T(8,128)(2,1)} copy(bf16[2048,64]{0,1:T(8,128)(2,1)} %bitcast.2) | data formatting | bytes 524288
  78.3 1.7 %copy.8 = bf16[32,4096]{1,0:T(8,128)(2,1)} copy(bf16[32,4096]{1,0:T(8,128)(2,1)} %get-tuple-element.9) | data formatting | bytes 524288
